TPU v7x, 32 devices: a whole 2x2x4 slice. The times are simulated.
32 devices in a mesh: pipe: 2 (over x), fsdp: 8 (over z, y), rep: 2 (over core).
Axes of the slice: x: 2, y: 2, z: 4, core: 2. Of those that a mesh axis runs over, the one named last changes fastest.
Arguments:
- section_acts: bfloat16 [2, 2, 1024, 3072], P('pipe', 'rep', 'fsdp'), may hold values from -6 to 6
- route_ids: int32 [2, 2, 1024, 2], P('pipe', 'rep', 'fsdp'), may hold values from 0 to 7, as said below
- gate_weight: bfloat16 [2, 3072, 8192], P('pipe', None, 'fsdp'), may hold values from -0.109375 to 0.109375
- hidden_cot: bfloat16 [2, 2, 192, 8192], P('pipe', 'rep', None, 'fsdp'), may hold values from -6 to 6
Outputs:
- weight_grad: bfloat16 [2, 3072, 8192], P('pipe', 'rep', 'fsdp')
- acts_grad: bfloat16 [2, 2, 1024, 3072], P('pipe', 'rep', 'fsdp')
Inputs may be any that keep to these rules, and one draw needn't show every extreme that they name: `route_ids`: in every section, replica and block of 128 consecutive tokens at most 24 tokens name expert 0, and in every section and replica some block has exactly 24; a token's two ids differ.
All inputs are finite; a program needn't handle non-finite values.
Results may differ from a plain program's by a relative error of at most 0.0059.
Values may be sent and summed in bfloat16 or wider, within the bound.
A program may use at most 128 MiB of HBM per device.

v0:
```python
import jax
import jax.numpy as jnp
from jax import lax
from jax.sharding import PartitionSpec as P


def from_behind(block, axis, distance):
    devices = range(lax.axis_size(axis))
    route = [((i - distance) % len(devices), i) for i in devices]
    return lax.ppermute(block, axis, route)


def slot_pick(route_block, capacity):
    chosen = jnp.any(route_block == 0, axis=-1)
    ordinal = jnp.cumsum(chosen.astype(jnp.int32)) - 1
    slot_ids = jnp.arange(capacity, dtype=jnp.int32)
    hits = (ordinal[None, :] == slot_ids[:, None]) & chosen[None, :]
    return hits.astype(jnp.bfloat16)


def compact(picker, inputs):
    return jnp.dot(picker, inputs, preferred_element_type=jnp.float32).astype(jnp.bfloat16)


def expand(picker, slot_grad):
    spread = lax.dot_general(
        picker, slot_grad, (((0,), (0,)), ((), ())), preferred_element_type=jnp.float32
    )
    return spread.astype(jnp.bfloat16)


def per_device(section_acts, route_ids, gate_weight, hidden_cot):
    inputs = section_acts[0, 0]
    routes = route_ids[0, 0]
    weight = gate_weight[0]
    cotangent = hidden_cot[0, 0]
    blocks = lax.axis_size("fsdp")
    capacity = cotangent.shape[0] // blocks
    previous = from_behind(inputs, "pipe", 1)
    picker = slot_pick(routes, capacity)
    routed = compact(picker, previous)
    gathered = lax.all_gather(routed, "fsdp", axis=0, tiled=True)
    pre_act = jnp.dot(gathered, weight, preferred_element_type=jnp.float32)
    sig_val = jax.nn.sigmoid(pre_act)
    pre_grad = (cotangent.astype(jnp.float32) * sig_val * (1.0 + pre_act * (1.0 - sig_val))).astype(
        jnp.bfloat16
    )
    replica_term = lax.dot_general(
        gathered, pre_grad, (((0,), (0,)), ((), ())), preferred_element_type=jnp.float32
    )
    weight_grad = lax.psum_scatter(
        replica_term.astype(jnp.bfloat16), "rep", scatter_dimension=0, tiled=True
    )
    width = weight.shape[0]
    slot_term = lax.dot_general(
        pre_grad, weight, (((1,), (1,)), ((), ())), preferred_element_type=jnp.float32
    )
    slot_term = slot_term.reshape(blocks, capacity, width)
    received = lax.all_to_all(slot_term, "fsdp", split_axis=0, concat_axis=0, tiled=True)
    slot_grad = jnp.sum(received, axis=0).astype(jnp.bfloat16)
    acts_grad = from_behind(expand(picker, slot_grad), "pipe", -1)
    return (weight_grad[None], acts_grad[None, None])


def solution(mesh):
    return jax.shard_map(
        per_device,
        mesh=mesh,
        in_specs=(
            P("pipe", "rep", "fsdp", None),
            P("pipe", "rep", "fsdp", None),
            P("pipe", None, "fsdp"),
            P("pipe", "rep", None, "fsdp"),
        ),
        out_specs=(P("pipe", "rep", "fsdp"), P("pipe", "rep", "fsdp", None)),
        check_vma=False,
    )
```

profile of v0, /device:TPU:0, one launch (start us, length us, event | category | flops | bytes accessed | tf_op | source)
XLA Modules:
  0.0 168.0 jit_solution(1970369880420399312)
XLA Ops:
  7.2 0.0 all-gather.2.cloned.1.call-start
  7.2 3.0 %collective-permute-start = (bf16[128,3072]{1,0:T(8,128)(2,1)}, bf16[128,3072]{1,0:T(8,128)(2,1)S(1)}, u32[]{:S(2)}, u32[]{:S(2)}) collective-permute-start(bf16[128,3072]{1,0:T(8,128)(2,1)} %bitcast.26), channel_id=1, source_target_pairs={{16,0},{0,16},{17,1},{1,17},{18,2},{2,18},{19,3},{3,19},{20,4},{4,... | collective-permute-start | bytes 2359304 | tf_op jit(solution)/shard_map/ppermute | solution.py:10
  10.2 0.7 compare_reduce_fusion
  10.9 0.1 copy.8
  11.0 0.2 reduce-window.8
  11.2 0.1 add_reduce_fusion
  11.3 16.7 %collective-permute-done = bf16[128,3072]{1,0:T(8,128)(2,1)S(1)} collective-permute-done((bf16[128,3072]{1,0:T(8,128)(2,1)}, bf16[128,3072]{1,0:T(8,128)(2,1)S(1)}, u32[]{:S(2)}, u32[]{:S(2)}) %collective-permute-start) | collective-permute-done | bytes 786464 | tf_op jit(solution)/shard_map/ppermute | solution.py:10
  28.0 0.9 convolution_convert_fusion.2
  28.8 0.0 all-gather.2.cloned.1.call-update
  28.9 0.0 reduce-scatter.2.cloned.1.call-start
  28.9 42.7 %all-gather.2.cloned.1.call-done = bf16[192,3072]{1,0:T(8,128)(2,1)} async-done(((bf16[24,3072]{1,0:T(8,128)(2,1)}), bf16[192,3072]{1,0:T(8,128)(2,1)}) %all-gather.2.cloned.1.call-update) | async-done | bytes 1179664 | tf_op jit(solution)/shard_map/all_gather | solution.py:42
  71.6 0.0 copy-start
  71.6 4.9 %fusion.5 = bf16[192,1024]{1,0:T(8,128)(2,1)S(1)} fusion(bf16[192,3072]{1,0:T(8,128)(2,1)} %all-gather.2.cloned.1.call-done, bf16[1,3072,1024]{2,1,0:T(8,128)(2,1)} %param.6, bf16[1,1,192,1024]{3,2,1,0:T(8,128)(2,1)} %param.7), kind=kOutput, calls=%fused_computation.9 | convolution fusion | flops 1209925632 | bytes 8257536 | tf_op jit(solution)/shard_map/dot_general | solution.py:43
  76.5 0.0 copy-done
  76.5 4.5 %convolution_convert_fusion = bf16[3072,1024]{1,0:T(8,128)(2,1)} fusion(bf16[192,3072]{1,0:T(8,128)(2,1)S(1)} %copy-done, bf16[192,1024]{1,0:T(8,128)(2,1)S(1)} %fusion.5), kind=kOutput, calls=%fused_computation.4 | convolution fusion | flops 1211105280 | bytes 7864320 | tf_op jit(solution)/shard_map/dot_general | solution.py:48
  81.0 0.0 reduce-scatter.2.cloned.1.call-update
  81.0 5.0 %fusion = f32[8,24,3072]{2,1,0:T(8,128)S(1)} fusion(bf16[8,24,1024]{2,1,0:T(8,128)(2,1)S(1)} %bitcast.23, bf16[1,3072,1024]{2,1,0:T(8,128)(2,1)} %param.6), kind=kOutput, calls=%fused_computation | convolution fusion | flops 1207959552 | bytes 9043968 | tf_op jit(solution)/shard_map/dot_general | solution.py:55
  86.0 55.8 %all_to_all.5 = f32[8,24,3072]{2,1,0:T(8,128)S(1)} all-to-all(f32[8,24,3072]{2,1,0:T(8,128)S(1)} %fusion), channel_id=1, replica_groups=mesh['pipe'=2,'fsdp'=8,'rep'=2] {'fsdp'}, dimensions={0} | all-to-all | bytes 4718592 | tf_op jit(solution)/shard_map/all_to_all | solution.py:59
  141.8 0.1 reduce_sum.9
  141.9 0.4 convolution_convert_fusion.1
  142.3 1.6 collective-permute-start.1
  143.9 16.4 %collective-permute-done.1 = bf16[128,3072]{1,0:T(8,128)(2,1)S(1)} collective-permute-done((bf16[128,3072]{1,0:T(8,128)(2,1)S(1)}, bf16[128,3072]{1,0:T(8,128)(2,1)S(1)}, u32[]{:S(2)}, u32[]{:S(2)}) %collective-permute-start.1) | collective-permute-done | bytes 786464 | tf_op jit(solution)/shard_map/ppermute | solution.py:10
  160.3 0.0 reduce-scatter.2.cloned.1.call-done
  160.3 0.9 copy.10
  (1 shorter events, 0.0 us)
Async XLA Ops:
  7.2 64.4 %all-gather.2.cloned.1.call-start = ((), (), s32[]{:S(2)}) async-start(), calls=%async_computation.2 | async-start | bytes 1327104 | tf_op jit(solution)/shard_map/all_gather | solution.py:42
  7.2 20.8 %collective-permute-start = (bf16[128,3072]{1,0:T(8,128)(2,1)}, bf16[128,3072]{1,0:T(8,128)(2,1)S(1)}, u32[]{:S(2)}, u32[]{:S(2)}) collective-permute-start(bf16[128,3072]{1,0:T(8,128)(2,1)} %bitcast.26), channel_id=1, source_target_pairs={{16,0},{0,16},{17,1},{1,17},{18,2},{2,18},{19,3},{3,19},{20,4},{4,... | collective-permute-start | bytes 2359304 | tf_op jit(solution)/shard_map/ppermute | solution.py:10
  28.9 131.4 %reduce-scatter.2.cloned.1.call-start = ((), (), s32[]{:S(2)}) async-start(), calls=%async_computation.3 | async-start | bytes 9437184 | tf_op jit(solution)/shard_map/reduce_scatter | solution.py:51
  71.6 4.9 %copy-start = (bf16[192,3072]{1,0:T(8,128)(2,1)S(1)}, bf16[192,3072]{1,0:T(8,128)(2,1)}, u32[]{:S(2)}) copy-start(bf16[192,3072]{1,0:T(8,128)(2,1)} %all-gather.2.cloned.1.call-done) | copy-start | bytes 3538948
  142.3 18.0 %collective-permute-start.1 = (bf16[128,3072]{1,0:T(8,128)(2,1)S(1)}, bf16[128,3072]{1,0:T(8,128)(2,1)S(1)}, u32[]{:S(2)}, u32[]{:S(2)}) collective-permute-start(bf16[128,3072]{1,0:T(8,128)(2,1)S(1)} %convolution_convert_fusion.1), channel_id=1, source_target_pairs={{16,0},{0,16},{17,1},{1,17},{18,2},{2,18},{19,3},{3,19},{20,4},{4,... | collective-permute-start | bytes 2359304 | tf_op jit(solution)/shard_map/ppermute | solution.py:10
Sparse Core Ops, SparseCore 0:
  29.0 42.5 all-gather.1
  81.1 13.2 reduce-scatter.1
where the time goes:
time: 168 us
  waiting for transfers between devices  75.8 us (45%)
  blocking collectives  55.8 us (33%)
  matrix products  15.6 us (9%)
  between operations  14.1 us (8%)
  starting transfers between devices  4.64 us (3%)
    all_to_all x1, blocking collectives, per_device(): lax.all_to_all(slot_term, 'fsdp', split_axis=0, concat_axis=0, tiled=True)  55.8 us
    all_gather x1, waiting for transfers between devices, per_device(): gathered = lax.all_gather(routed, 'fsdp', axis=0, tiled=True)  42.7 us
    ppermute x2, waiting for transfers between devices, from_behind(): return lax.ppermute(block, axis, route)  33.1 us
    dot_general x1, matrix products, per_device(): lax.dot_general(pre_grad, weight, (((1,), (1,)), ((), ())), preferred_ele...  4.97 us
    dot_general x1, matrix products, per_device(): pre_act = jnp.dot(gathered, weight, preferred_element_type=jnp.float32)  4.86 us
    ppermute x2, starting transfers between devices, from_behind(): return lax.ppermute(block, axis, route)  4.56 us
    dot_general x1, matrix products, per_device(): lax.dot_general(gathered, pre_grad, (((0,), (0,)), ((), ())), preferred_e...  4.52 us
  transfers between devices with their start and end apart: 4, of which 3 were waited for; matrix products, arithmetic and copies ran while one was open for 4% of the time, Pallas kernels for 0%

commit v1 on v0

v1 whole, which is shorter than its diff:
```python
import functools

import jax
import jax.numpy as jnp
from jax import lax
from jax.experimental import pallas as pl
from jax.experimental.pallas import tpu as pltpu
from jax.sharding import PartitionSpec as P

MESH = pl.DeviceIdType.MESH
F32 = jnp.float32
BF16 = jnp.bfloat16
CHUNKS = 4


def factors(n):
    fast = 1
    while (fast * 2) ** 2 <= n:
        fast *= 2
    return n // fast, fast


def kernel(
    n, pipe, cap,
    routes_hbm, acts_hbm, weight_hbm, cot_hbm,
    wgrad_hbm, agrad_hbm,
    ids, acts, weight, cot, compacted, gathered, rows, acc, pre_grad,
    own_term, y_out, y_in, z_out, up_in, down_in, total, done, back, spread,
    w_out, w_in, w_sum,
    local_sem, ids_sem, x_send, g_recv, g_send, y_send, y_recv, z_send, z_recv,
    b_send, b_recv, w_send, w_recv, o_sem,
):
    chunks = CHUNKS
    slow, fast = factors(n)
    p, f, r = lax.axis_index("pipe"), lax.axis_index("fsdp"), lax.axis_index("rep")
    a, b = f // fast, lax.rem(f, fast)
    nxt, prv = lax.rem(p + 1, pipe), lax.rem(p + pipe - 1, pipe)
    slots = n * cap
    dc = weight.shape[1]
    half = chunks // 2
    has_up, has_down = a < slow - 1, a > 0
    up, down = (a + 1) * fast + b, (a - 1) * fast + b

    def peer(j):
        return a * fast + lax.rem(b + j, fast)

    def remote(src, dst, send, recv, where):
        return pltpu.make_async_remote_copy(
            src_ref=src, dst_ref=dst, send_sem=send, recv_sem=recv,
            device_id=where, device_id_type=MESH,
        )

    def greet(where):
        pl.semaphore_signal(barrier, inc=1, device_id=where, device_id_type=MESH)

    acts_load = pltpu.make_async_copy(acts_hbm, acts, local_sem.at[0])
    acts_load.start()
    barrier = pltpu.get_barrier_semaphore()
    greet({"pipe": prv})
    if pipe > 2:
        greet({"pipe": nxt})
    greet({"rep": 1 - r})
    for j in range(1, fast):
        greet({"fsdp": peer(j)})

    @pl.when(has_up)
    def _():
        greet({"fsdp": up})

    @pl.when(has_down)
    def _():
        greet({"fsdp": down})

    weight_loads = []
    for c in range(chunks):
        load = pltpu.make_async_copy(
            weight_hbm.at[pl.ds(c * dc, dc)], weight.at[c], local_sem.at[2 + c]
        )
        load.start()
        weight_loads.append(load)
    cot_load = pltpu.make_async_copy(cot_hbm, cot, local_sem.at[1])
    cot_load.start()

    greeted = (1 if pipe == 2 else 2) + 1 + (fast - 1)
    pl.semaphore_wait(
        barrier, greeted + has_up.astype(jnp.int32) + has_down.astype(jnp.int32)
    )

    ids_copy = remote(routes_hbm, ids, ids_sem.at[0], ids_sem.at[1], {"pipe": prv})
    ids_copy.start()
    ids_copy.wait_recv()
    tokens = ids.shape[1]
    named = jnp.where(ids[...] == 0, 1.0, 0.0).astype(F32)
    chosen = jnp.max(named, axis=0, keepdims=True)
    row = lax.broadcasted_iota(jnp.int32, (tokens, tokens), 0)
    col = lax.broadcasted_iota(jnp.int32, (tokens, tokens), 1)
    before = jnp.where(row <= col, 1.0, 0.0).astype(BF16)
    chosen8 = jnp.broadcast_to(chosen, (16, tokens))
    ordinal = jnp.dot(chosen8.astype(BF16), before, preferred_element_type=F32)[0:1] - 1.0
    hits = jnp.where(
        (jnp.broadcast_to(ordinal, (tokens, tokens)) == row.astype(F32))
        & (jnp.broadcast_to(chosen, (tokens, tokens)) > 0.5),
        1.0, 0.0,
    ).astype(F32)
    picker = hits[0:cap].astype(BF16)
    spreader = hits.T.astype(BF16)
    acts_load.wait()

    def x_copy(c):
        return remote(
            compacted.at[c], gathered.at[c, f], x_send.at[c], g_recv.at[c, f], {"pipe": nxt}
        )

    for c in range(chunks):
        compacted[c] = jnp.dot(
            picker, acts[:, c * dc:(c + 1) * dc], preferred_element_type=F32
        ).astype(BF16)
        x_copy(c).start()

    def g_copy(c, origin, kind, where):
        block = origin * fast + b
        return remote(
            gathered.at[c, block], gathered.at[c, block],
            g_send.at[c, origin, kind], g_recv.at[c, block], {"fsdp": where},
        )

    def g_wait(c, block):
        remote(
            gathered.at[c, block], gathered.at[c, block],
            g_send.at[c, 0, 0], g_recv.at[c, block], {"pipe": nxt},
        ).wait_recv()

    def g_fan(c, origin, act):
        for j in range(1, fast):
            act(g_copy(c, origin, 1 + j, peer(j)))

    def g_step(c, k, act, wait):
        if k == 0:
            if wait:
                g_wait(c, f)

            @pl.when(has_up)
            def _():
                act(g_copy(c, a, 0, up))

            @pl.when(has_down)
            def _():
                act(g_copy(c, a, 1, down))

            g_fan(c, a, act)
            return

        @pl.when(a - k >= 0)
        def _():
            if wait:
                g_wait(c, (a - k) * fast + b)

            @pl.when(has_up)
            def _():
                act(g_copy(c, a - k, 0, up))

            g_fan(c, a - k, act)

        @pl.when(a + k < slow)
        def _():
            if wait:
                g_wait(c, (a + k) * fast + b)

            @pl.when(has_down)
            def _():
                act(g_copy(c, a + k, 1, down))

            g_fan(c, a + k, act)

    def first_matmul(c):
        for origin in range(slow):
            for j in range(1, fast):
                g_wait(c, origin * fast + lax.rem(b + j, fast))
        block = gathered[c].astype(F32).reshape(slots, dc).astype(BF16)
        rows[c] = block
        weight_loads[c].wait()
        part = jnp.dot(block, weight[c], preferred_element_type=F32)
        if c == 0:
            acc[...] = part
        else:
            acc[...] += part

    for t in range(chunks + slow - 1):
        for c in range(chunks):
            if 0 <= t - c < slow:
                g_step(c, t - c, lambda copy: copy.start(), True)
        c = t - slow + 1
        if c >= 0:
            first_matmul(c)

    cot_load.wait()
    piece = 48
    for i in range(slots // piece):
        span = pl.ds(i * piece, piece)
        pre = acc[span]
        s = jax.nn.sigmoid(pre)
        pre_grad[span] = (cot[span].astype(F32) * s * (1.0 + pre * (1.0 - s))).astype(BF16)

    def y_copy(c, j):
        to = lax.rem(b + j, fast)
        return remote(
            y_out.at[c, to], y_in.at[c, j - 1], y_send.at[c, j - 1], y_recv.at[c, j - 1],
            {"fsdp": peer(j)},
        )

    def slot_matmul(c):
        term = lax.dot_general(
            pre_grad[...], weight[c], (((1,), (1,)), ((), ())), preferred_element_type=F32
        ).reshape(n, cap, dc)
        own_term[c] = term
        for aa in range(slow):
            for bb in range(fast):
                y_out[c, bb, aa] = term[aa * fast + bb].astype(BF16)
        for j in range(1, fast):
            y_copy(c, j).start()

    def partial(c, dest):
        value = own_term[c, dest * fast + b]
        for j in range(1, fast):
            value = value + y_in[c, j - 1, dest].astype(F32)
        return value

    def z_copy(c, dest, way):
        landing = up_in if way == 0 else down_in
        return remote(
            z_out.at[c, dest], landing.at[c, dest], z_send.at[c, dest],
            z_recv.at[way, c, dest], {"fsdp": up if way == 0 else down},
        )

    def z_wait(c, dest, way):
        z_copy(c, dest, way).wait_recv()

    def line(c, dest, way):
        landing = up_in if way == 0 else down_in
        middle = has_down if way == 0 else has_up

        @pl.when(middle)
        def _():
            z_wait(c, dest, way)
            z_out[c, dest] = (partial(c, dest) + landing[c, dest].astype(F32)).astype(BF16)

        @pl.when(jnp.logical_not(middle))
        def _():
            z_out[c, dest] = partial(c, dest).astype(BF16)

        z_copy(c, dest, way).start()

    def back_copy(c):
        return remote(done.at[c], back.at[c], b_send.at[c], b_recv.at[c], {"pipe": prv})

    def r_step(c, k):
        if k == 0:
            for j in range(1, fast):
                y_copy(c, j).wait_recv()
        if k < slow - 1:
            top, bottom = slow - 1 - k, k

            @pl.when(top > a)
            def _():
                line(c, top, 0)

            @pl.when(bottom < a)
            def _():
                line(c, bottom, 1)

            return
        total[...] = partial(c, a)

        @pl.when(has_down)
        def _():
            z_wait(c, a, 0)
            total[...] += up_in[c, a].astype(F32)

        @pl.when(has_up)
        def _():
            z_wait(c, a, 1)
            total[...] += down_in[c, a].astype(F32)

        done[c] = total[...].astype(BF16)
        back_copy(c).start()

    def weight_tile(index):
        return lax.dot_general(
            rows[index], pre_grad[...], (((0,), (0,)), ((), ())), preferred_element_type=F32
        ).astype(BF16)

    def w_copy(i):
        return remote(w_out.at[i], w_in.at[i], w_send.at[i], w_recv.at[i], {"rep": 1 - r})

    def other_half(i):
        w_out[i] = weight_tile((1 - r) * half + i)
        w_copy(i).start()

    def own_half(i):
        w_sum[i] = weight_tile(r * half + i)

    def w_store(i):
        return pltpu.make_async_copy(
            w_sum.at[i], wgrad_hbm.at[pl.ds(i * dc, dc)], o_sem.at[chunks + i]
        )

    def add_halves(i):
        w_copy(i).wait_recv()
        w_sum[i] = (w_sum[i].astype(F32) + w_in[i].astype(F32)).astype(BF16)
        w_store(i).start()

    def a_store(c):
        return pltpu.make_async_copy(
            spread.at[c], agrad_hbm.at[:, pl.ds(c * dc, dc)], o_sem.at[c]
        )

    def put_back(c):
        back_copy(c).wait_recv()
        grads = back[c].astype(F32)
        padded = jnp.concatenate(
            [grads, jnp.zeros((tokens - cap, dc), F32)], axis=0
        ).astype(BF16)
        spread[c] = jnp.dot(spreader, padded, preferred_element_type=F32).astype(BF16)
        a_store(c).start()

    for c in range(chunks):
        slot_matmul(c)
    beside = [functools.partial(other_half, i) for i in range(half)]
    beside += [functools.partial(own_half, i) for i in range(half)]
    beside += [functools.partial(add_halves, i) for i in range(half)]
    for t in range(chunks + slow - 1):
        for c in range(chunks):
            if 0 <= t - c < slow:
                r_step(c, t - c)
        if beside:
            beside.pop(0)()
    for act in beside:
        act()
    for c in range(chunks):
        put_back(c)

    ids_copy.wait_send()
    for c in range(chunks):
        x_copy(c).wait_send()
        for k in range(slow):
            g_step(c, k, lambda copy: copy.wait_send(), False)
        for j in range(1, fast):
            y_copy(c, j).wait_send()
        for dest in range(slow):

            @pl.when(dest != a)
            def _():
                z_copy(c, dest, 0).wait_send()

        back_copy(c).wait_send()
    for i in range(half):
        w_copy(i).wait_send()
        w_store(i).wait()
    for c in range(chunks):
        a_store(c).wait()


def per_device(section_acts, route_ids, gate_weight, hidden_cot):
    n, pipe = lax.axis_size("fsdp"), lax.axis_size("pipe")
    acts, weight, cot = section_acts[0, 0], gate_weight[0], hidden_cot[0, 0]
    routes = route_ids[0, 0].T
    tokens, width = acts.shape
    slots, hidden = cot.shape
    cap = slots // n
    slow, fast = factors(n)
    chunks, half = CHUNKS, CHUNKS // 2
    dc = width // chunks
    peers = max(fast - 1, 1)
    dma = pltpu.SemaphoreType.DMA
    vm = pltpu.VMEM
    scratch = [
        vm(routes.shape, jnp.int32),
        vm((tokens, width), BF16),
        vm((chunks, dc, hidden), BF16),
        vm((slots, hidden), BF16),
        vm((chunks, cap, dc), BF16),
        vm((chunks, n, cap, dc), BF16),
        vm((chunks, slots, dc), BF16),
        vm((slots, hidden), F32),
        vm((slots, hidden), BF16),
        vm((chunks, n, cap, dc), F32),
        vm((chunks, fast, slow, cap, dc), BF16),
        vm((chunks, peers, slow, cap, dc), BF16),
        vm((chunks, slow, cap, dc), BF16),
        vm((chunks, slow, cap, dc), BF16),
        vm((chunks, slow, cap, dc), BF16),
        vm((cap, dc), F32),
        vm((chunks, cap, dc), BF16),
        vm((chunks, cap, dc), BF16),
        vm((chunks, tokens, dc), BF16),
        vm((half, dc, hidden), BF16),
        vm((half, dc, hidden), BF16),
        vm((half, dc, hidden), BF16),
        dma((2 + chunks,)),
        dma((2,)),
        dma((chunks,)),
        dma((chunks, n)),
        dma((chunks, slow, 1 + fast)),
        dma((chunks, peers)),
        dma((chunks, peers)),
        dma((chunks, slow)),
        dma((2, chunks, slow)),
        dma((chunks,)),
        dma((chunks,)),
        dma((half,)),
        dma((half,)),
        dma((chunks + half,)),
    ]
    anywhere = pl.BlockSpec(memory_space=pl.ANY)
    weight_grad, acts_grad = pl.pallas_call(
        functools.partial(kernel, n, pipe, cap),
        out_shape=(
            jax.ShapeDtypeStruct((width // 2, hidden), BF16),
            jax.ShapeDtypeStruct((tokens, width), BF16),
        ),
        in_specs=[anywhere] * 4,
        out_specs=(anywhere, anywhere),
        scratch_shapes=scratch,
        compiler_params=pltpu.CompilerParams(
            collective_id=0, has_side_effects=True, vmem_limit_bytes=56 * 1024 * 1024
        ),
        cost_estimate=pl.CostEstimate(
            flops=6 * slots * width * hidden,
            bytes_accessed=3 * width * hidden + 4 * tokens * width,
            transcendentals=slots * hidden,
        ),
    )(routes, acts, weight, cot)
    return (weight_grad[None], acts_grad[None, None])


def solution(mesh):
    return jax.shard_map(
        per_device,
        mesh=mesh,
        in_specs=(
            P("pipe", "rep", "fsdp", None),
            P("pipe", "rep", "fsdp", None),
            P("pipe", None, "fsdp"),
            P("pipe", "rep", None, "fsdp"),
        ),
        out_specs=(P("pipe", "rep", "fsdp"), P("pipe", "rep", "fsdp", None)),
        check_vma=False,
    )
```

time: 168 us -> 83.5 us (0.50)
  Pallas kernels: 0 us -> 77.9 us
  waiting for transfers between devices: 75.8 us -> 0 us
  blocking collectives: 55.8 us -> 0 us
  matrix products: 15.6 us -> 0 us
  between operations: 14.1 us -> 0.65 us
  starting transfers between devices: 4.64 us -> 0 us
  local copies, waits for them, and re-layouts: 1 us -> 4.81 us
    pallas_call x0 -> x1, Pallas kernels: none -> 77.9 us  [per_device(): pl.pallas_call(functools.partial(kernel, n, pipe, cap), out_shape=(jax.Sh...]
    all_to_all x1 -> x0, blocking collectives: 55.8 us -> none  [per_device(): lax.all_to_all(slot_term, 'fsdp', split_axis=0, concat_axis=0, tiled=True)]
    all_gather x1 -> x0, waiting for transfers between devices: 42.7 us -> none  [per_device(): gathered = lax.all_gather(routed, 'fsdp', axis=0, tiled=True)]
    ppermute x2 -> x0, waiting for transfers between devices: 33.1 us -> none  [from_behind(): return lax.ppermute(block, axis, route)]
    dot_general x5 -> x0, matrix products: 15.6 us -> none  [the longest x1 4.97 us: per_device(): lax.dot_general(pre_grad, weight, (((1,), (1,)), ((), ())), preferred_ele...]
    ppermute x2 -> x0, starting transfers between devices: 4.56 us -> none  [from_behind(): return lax.ppermute(block, axis, route)]
    unnamed x3 -> x4, local copies, waits for them, and re-layouts: 0.88 us -> 4.81 us
  transfers between devices with their start and end apart: 4 -> 0, of which waited for: 3 -> 0; matrix products, arithmetic and copies ran while one was open for 4% -> 0% of each run, Pallas kernels for 0% -> 0%
where the time goes in v1:
time: 83.5 us; the launch traced here: 83.4 us
  Pallas kernels  77.9 us (93%)
  local copies, waits for them, and re-layouts  4.81 us (6%)
    pallas_call x1, Pallas kernels, per_device(): pl.pallas_call(functools.partial(kernel, n, pipe, cap), out_shape=(jax.Sh...  77.9 us
    unnamed x4, local copies, waits for them, and re-layouts  4.81 us

profile of v1, /device:TPU:0, one launch (start us, length us, event | category | flops | bytes accessed | tf_op | source)
XLA Modules:
  0.0 83.4 jit_solution(52232193834628589)
XLA Ops:
  0.6 77.9 %shard_map.59 = (bf16[1536,1024]{1,0:T(8,128)(2,1)}, bf16[128,3072]{1,0:T(8,128)(2,1)}) custom-call(s32[2,128]{1,0:T(2,128)} %bitcast.13, bf16[128,3072]{1,0:T(8,128)(2,1)} %bitcast.11, bf16[3072,1024]{1,0:T(8,128)(2,1)} %bitcast.10, bf16[192,1024]{1,0:T(8,128)(2,1)} %bitcast.12), custom_call_target="tpu_custom_call" | custom-call | flops 3623878656 | bytes 11010048 | tf_op jit(solution)/shard_map/pallas_call | solution.py:415
  78.6 0.0 copy-start
  78.6 3.9 %copy.8 = bf16[1,1536,1024]{2,1,0:T(8,128)(2,1)} copy(bf16[1,1536,1024]{2,1,0:T(8,128)(2,1)} %bitcast.8) | data formatting | bytes 6291456
  82.5 0.0 copy-done
  82.5 0.9 %copy.9 = bf16[1,1,128,3072]{3,2,1,0:T(8,128)(2,1)} copy(bf16[1,1,128,3072]{3,2,1,0:T(8,128)(2,1)S(1)} %bitcast.9) | data formatting | bytes 1572864
Async XLA Ops:
  78.6 3.9 %copy-start = (bf16[128,3072]{1,0:T(8,128)(2,1)S(1)}, bf16[128,3072]{1,0:T(8,128)(2,1)}, u32[]{:S(2)}) copy-start(bf16[128,3072]{1,0:T(8,128)(2,1)} %get-tuple-element.5) | copy-start | bytes 2359300

commit v2 on v1

--- a/solution.py
+++ b/solution.py
@@ -23,12 +23,12 @@
 def kernel(
     n, pipe, cap,
     routes_hbm, acts_hbm, weight_hbm, cot_hbm,
-    wgrad_hbm, agrad_hbm,
+    w_sum, spread,
     ids, acts, weight, cot, compacted, gathered, rows, acc, pre_grad,
-    own_term, y_out, y_in, z_out, up_in, down_in, total, done, back, spread,
-    w_out, w_in, w_sum,
+    own_term, y_out, y_in, z_out, up_in, down_in, total, done, back,
+    w_out, w_in,
     local_sem, ids_sem, x_send, g_recv, g_send, y_send, y_recv, z_send, z_recv,
-    b_send, b_recv, w_send, w_recv, o_sem,
+    b_send, b_recv, w_send, w_recv,
 ):
     chunks = CHUNKS
     slow, fast = factors(n)
@@ -185,12 +185,10 @@
         else:
             acc[...] += part
 
-    for t in range(chunks + slow - 1):
-        for c in range(chunks):
-            if 0 <= t - c < slow:
-                g_step(c, t - c, lambda copy: copy.start(), True)
-        c = t - slow + 1
-        if c >= 0:
+    steps = sorted((c + 2 * k, k, c) for c in range(chunks) for k in range(slow))
+    for _, k, c in steps:
+        g_step(c, k, lambda copy: copy.start(), True)
+        if k == slow - 1:
             first_matmul(c)
 
     cot_load.wait()
@@ -201,11 +199,11 @@
         s = jax.nn.sigmoid(pre)
         pre_grad[span] = (cot[span].astype(F32) * s * (1.0 + pre * (1.0 - s))).astype(BF16)
 
-    def y_copy(c, j):
+    def y_copy(c, j, dest):
         to = lax.rem(b + j, fast)
         return remote(
-            y_out.at[c, to], y_in.at[c, j - 1], y_send.at[c, j - 1], y_recv.at[c, j - 1],
-            {"fsdp": peer(j)},
+            y_out.at[c, to, dest], y_in.at[c, j - 1, dest], y_send.at[c, j - 1, dest],
+            y_recv.at[c, j - 1, dest], {"fsdp": peer(j)},
         )
 
     def slot_matmul(c):
@@ -216,12 +214,15 @@
         for aa in range(slow):
             for bb in range(fast):
                 y_out[c, bb, aa] = term[aa * fast + bb].astype(BF16)
-        for j in range(1, fast):
-            y_copy(c, j).start()
+        far_first = sorted(range(slow), key=lambda dest: -abs(2 * dest - slow + 1))
+        for dest in far_first:
+            for j in range(1, fast):
+                y_copy(c, j, dest).start()
 
     def partial(c, dest):
         value = own_term[c, dest * fast + b]
         for j in range(1, fast):
+            y_copy(c, j, dest).wait_recv()
             value = value + y_in[c, j - 1, dest].astype(F32)
         return value
 
@@ -254,9 +255,6 @@
         return remote(done.at[c], back.at[c], b_send.at[c], b_recv.at[c], {"pipe": prv})
 
     def r_step(c, k):
-        if k == 0:
-            for j in range(1, fast):
-                y_copy(c, j).wait_recv()
         if k < slow - 1:
             top, bottom = slow - 1 - k, k
 
@@ -299,20 +297,9 @@
     def own_half(i):
         w_sum[i] = weight_tile(r * half + i)
 
-    def w_store(i):
-        return pltpu.make_async_copy(
-            w_sum.at[i], wgrad_hbm.at[pl.ds(i * dc, dc)], o_sem.at[chunks + i]
-        )
-
     def add_halves(i):
         w_copy(i).wait_recv()
         w_sum[i] = (w_sum[i].astype(F32) + w_in[i].astype(F32)).astype(BF16)
-        w_store(i).start()
-
-    def a_store(c):
-        return pltpu.make_async_copy(
-            spread.at[c], agrad_hbm.at[:, pl.ds(c * dc, dc)], o_sem.at[c]
-        )
 
     def put_back(c):
         back_copy(c).wait_recv()
@@ -320,33 +307,34 @@
         padded = jnp.concatenate(
             [grads, jnp.zeros((tokens - cap, dc), F32)], axis=0
         ).astype(BF16)
-        spread[c] = jnp.dot(spreader, padded, preferred_element_type=F32).astype(BF16)
-        a_store(c).start()
-
-    for c in range(chunks):
-        slot_matmul(c)
+        spread[:, c * dc:(c + 1) * dc] = jnp.dot(
+            spreader, padded, preferred_element_type=F32
+        ).astype(BF16)
+
     beside = [functools.partial(other_half, i) for i in range(half)]
     beside += [functools.partial(own_half, i) for i in range(half)]
-    beside += [functools.partial(add_halves, i) for i in range(half)]
-    for t in range(chunks + slow - 1):
+    for t in range(-2, chunks + slow - 1):
+        if 0 <= t + 2 < chunks:
+            slot_matmul(t + 2)
         for c in range(chunks):
             if 0 <= t - c < slow:
                 r_step(c, t - c)
         if beside:
             beside.pop(0)()
-    for act in beside:
-        act()
-    for c in range(chunks):
+    for c in range(chunks - 1):
         put_back(c)
+    for i in range(half):
+        add_halves(i)
+    put_back(chunks - 1)
 
     ids_copy.wait_send()
     for c in range(chunks):
         x_copy(c).wait_send()
         for k in range(slow):
             g_step(c, k, lambda copy: copy.wait_send(), False)
-        for j in range(1, fast):
-            y_copy(c, j).wait_send()
         for dest in range(slow):
+            for j in range(1, fast):
+                y_copy(c, j, dest).wait_send()
 
             @pl.when(dest != a)
             def _():
@@ -355,9 +343,6 @@
         back_copy(c).wait_send()
     for i in range(half):
         w_copy(i).wait_send()
-        w_store(i).wait()
-    for c in range(chunks):
-        a_store(c).wait()
 
 
 def per_device(section_acts, route_ids, gate_weight, hidden_cot):
@@ -392,8 +377,6 @@
         vm((cap, dc), F32),
         vm((chunks, cap, dc), BF16),
         vm((chunks, cap, dc), BF16),
-        vm((chunks, tokens, dc), BF16),
-        vm((half, dc, hidden), BF16),
         vm((half, dc, hidden), BF16),
         vm((half, dc, hidden), BF16),
         dma((2 + chunks,)),
@@ -401,25 +384,25 @@
         dma((chunks,)),
         dma((chunks, n)),
         dma((chunks, slow, 1 + fast)),
-        dma((chunks, peers)),
-        dma((chunks, peers)),
+        dma((chunks, peers, slow)),
+        dma((chunks, peers, slow)),
         dma((chunks, slow)),
         dma((2, chunks, slow)),
         dma((chunks,)),
         dma((chunks,)),
         dma((half,)),
         dma((half,)),
-        dma((chunks + half,)),
     ]
     anywhere = pl.BlockSpec(memory_space=pl.ANY)
+    inside = pl.BlockSpec(memory_space=pltpu.VMEM)
     weight_grad, acts_grad = pl.pallas_call(
         functools.partial(kernel, n, pipe, cap),
         out_shape=(
-            jax.ShapeDtypeStruct((width // 2, hidden), BF16),
-            jax.ShapeDtypeStruct((tokens, width), BF16),
+            vm((half, dc, hidden), BF16),
+            vm((tokens, width), BF16),
         ),
         in_specs=[anywhere] * 4,
-        out_specs=(anywhere, anywhere),
+        out_specs=(inside, inside),
         scratch_shapes=scratch,
         compiler_params=pltpu.CompilerParams(
             collective_id=0, has_side_effects=True, vmem_limit_bytes=56 * 1024 * 1024
@@ -430,7 +413,7 @@
             transcendentals=slots * hidden,
         ),
     )(routes, acts, weight, cot)
-    return (weight_grad[None], acts_grad[None, None])
+    return (weight_grad.reshape(1, width // 2, hidden), acts_grad[None, None])
 
 
 def solution(mesh):

time: 83.5 us -> 80.6 us (0.965)
  local copies, waits for them, and re-layouts: 4.81 us -> 2.55 us
    unnamed x4 -> x2, local copies, waits for them, and re-layouts: 4.81 us -> 2.55 us
where the time goes in v2:
time: 80.6 us; the launch traced here: 80.4 us
  Pallas kernels  77.3 us (96%)
  local copies, waits for them, and re-layouts  2.55 us (3%)
    pallas_call x1, Pallas kernels, per_device(): pl.pallas_call(functools.partial(kernel, n, pipe, cap), out_shape=(vm((ha...  77.3 us
    unnamed x2, local copies, waits for them, and re-layouts  2.55 us

profile of v2, /device:TPU:0, one launch (start us, length us, event | category | flops | bytes accessed | tf_op | source)
XLA Modules:
  0.0 80.4 jit_solution(6109831749925764486)
XLA Ops:
  0.6 77.3 %shard_map.59 = (bf16[2,768,1024]{2,1,0:T(8,128)(2,1)S(1)}, bf16[128,3072]{1,0:T(8,128)(2,1)S(1)}) custom-call(s32[2,128]{1,0:T(2,128)} %bitcast.13, bf16[128,3072]{1,0:T(8,128)(2,1)} %bitcast.11, bf16[3072,1024]{1,0:T(8,128)(2,1)} %bitcast.10, bf16[192,1024]{1,0:T(8,128)(2,1)} %bitcast.12), custom_call_target="tpu_custom_call" | custom-call | flops 3623878656 | bytes 11010048 | tf_op jit(solution)/shard_map/pallas_call | solution.py:398
  77.9 1.7 %copy.8 = bf16[1,1536,1024]{2,1,0:T(8,128)(2,1)} copy(bf16[1,1536,1024]{2,1,0:T(8,128)(2,1)S(1)} %bitcast.8) | data formatting | bytes 6291456
  79.6 0.9 %copy.9 = bf16[1,1,128,3072]{3,2,1,0:T(8,128)(2,1)} copy(bf16[1,1,128,3072]{3,2,1,0:T(8,128)(2,1)S(1)} %bitcast.9) | data formatting | bytes 1572864

commit v3 on v2

--- a/solution.py
+++ b/solution.py
@@ -24,11 +24,10 @@
     n, pipe, cap,
     routes_hbm, acts_hbm, weight_hbm, cot_hbm,
     w_sum, spread,
-    ids, acts, weight, cot, compacted, gathered, rows, acc, pre_grad,
+    ids, acts, weight, cot, compacted, gathered, rows, rows_out, acc, pre_grad,
     own_term, y_out, y_in, z_out, up_in, down_in, total, done, back,
-    w_out, w_in,
     local_sem, ids_sem, x_send, g_recv, g_send, y_send, y_recv, z_send, z_recv,
-    b_send, b_recv, w_send, w_recv,
+    b_send, b_recv, f_send, f_recv,
 ):
     chunks = CHUNKS
     slow, fast = factors(n)
@@ -172,12 +171,29 @@
 
             g_fan(c, a + k, act)
 
+    def rows_copy(i):
+        return remote(rows_out.at[i], rows.at[i, 1], f_send.at[i], f_recv.at[i], {"rep": 1 - r})
+
+    grad_copy = remote(
+        pre_grad.at[0], pre_grad.at[1], f_send.at[half], f_recv.at[half], {"rep": 1 - r}
+    )
+
     def first_matmul(c):
         for origin in range(slow):
             for j in range(1, fast):
                 g_wait(c, origin * fast + lax.rem(b + j, fast))
         block = gathered[c].astype(F32).reshape(slots, dc).astype(BF16)
-        rows[c] = block
+        i, mine = c % half, r == c // half
+
+        @pl.when(mine)
+        def _():
+            rows[i, 0] = block
+
+        @pl.when(jnp.logical_not(mine))
+        def _():
+            rows_out[i] = block
+            rows_copy(i).start()
+
         weight_loads[c].wait()
         part = jnp.dot(block, weight[c], preferred_element_type=F32)
         if c == 0:
@@ -197,7 +213,8 @@
         span = pl.ds(i * piece, piece)
         pre = acc[span]
         s = jax.nn.sigmoid(pre)
-        pre_grad[span] = (cot[span].astype(F32) * s * (1.0 + pre * (1.0 - s))).astype(BF16)
+        pre_grad[0, span] = (cot[span].astype(F32) * s * (1.0 + pre * (1.0 - s))).astype(BF16)
+    grad_copy.start()
 
     def y_copy(c, j, dest):
         to = lax.rem(b + j, fast)
@@ -208,7 +225,7 @@
 
     def slot_matmul(c):
         term = lax.dot_general(
-            pre_grad[...], weight[c], (((1,), (1,)), ((), ())), preferred_element_type=F32
+            pre_grad[0], weight[c], (((1,), (1,)), ((), ())), preferred_element_type=F32
         ).reshape(n, cap, dc)
         own_term[c] = term
         for aa in range(slow):
@@ -282,24 +299,14 @@
         done[c] = total[...].astype(BF16)
         back_copy(c).start()
 
-    def weight_tile(index):
-        return lax.dot_general(
-            rows[index], pre_grad[...], (((0,), (0,)), ((), ())), preferred_element_type=F32
+    def weight_tile(i):
+        if i == 0:
+            grad_copy.wait_recv()
+        rows_copy(i).wait_recv()
+        w_sum[i] = lax.dot_general(
+            rows[i].reshape(2 * slots, dc), pre_grad[...].reshape(2 * slots, -1),
+            (((0,), (0,)), ((), ())), preferred_element_type=F32,
         ).astype(BF16)
-
-    def w_copy(i):
-        return remote(w_out.at[i], w_in.at[i], w_send.at[i], w_recv.at[i], {"rep": 1 - r})
-
-    def other_half(i):
-        w_out[i] = weight_tile((1 - r) * half + i)
-        w_copy(i).start()
-
-    def own_half(i):
-        w_sum[i] = weight_tile(r * half + i)
-
-    def add_halves(i):
-        w_copy(i).wait_recv()
-        w_sum[i] = (w_sum[i].astype(F32) + w_in[i].astype(F32)).astype(BF16)
 
     def put_back(c):
         back_copy(c).wait_recv()
@@ -311,21 +318,17 @@
             spreader, padded, preferred_element_type=F32
         ).astype(BF16)
 
-    beside = [functools.partial(other_half, i) for i in range(half)]
-    beside += [functools.partial(own_half, i) for i in range(half)]
+    beside = [functools.partial(weight_tile, i) for i in range(half)]
     for t in range(-2, chunks + slow - 1):
         if 0 <= t + 2 < chunks:
             slot_matmul(t + 2)
         for c in range(chunks):
             if 0 <= t - c < slow:
                 r_step(c, t - c)
-        if beside:
+        if t >= 0 and beside:
             beside.pop(0)()
-    for c in range(chunks - 1):
+    for c in range(chunks):
         put_back(c)
-    for i in range(half):
-        add_halves(i)
-    put_back(chunks - 1)
 
     ids_copy.wait_send()
     for c in range(chunks):
@@ -342,7 +345,8 @@
 
         back_copy(c).wait_send()
     for i in range(half):
-        w_copy(i).wait_send()
+        rows_copy(i).wait_send()
+    grad_copy.wait_send()
 
 
 def per_device(section_acts, route_ids, gate_weight, hidden_cot):
@@ -365,9 +369,10 @@
         vm((slots, hidden), BF16),
         vm((chunks, cap, dc), BF16),
         vm((chunks, n, cap, dc), BF16),
-        vm((chunks, slots, dc), BF16),
+        vm((half, 2, slots, dc), BF16),
+        vm((half, slots, dc), BF16),
         vm((slots, hidden), F32),
-        vm((slots, hidden), BF16),
+        vm((2, slots, hidden), BF16),
         vm((chunks, n, cap, dc), F32),
         vm((chunks, fast, slow, cap, dc), BF16),
         vm((chunks, peers, slow, cap, dc), BF16),
@@ -377,8 +382,6 @@
         vm((cap, dc), F32),
         vm((chunks, cap, dc), BF16),
         vm((chunks, cap, dc), BF16),
-        vm((half, dc, hidden), BF16),
-        vm((half, dc, hidden), BF16),
         dma((2 + chunks,)),
         dma((2,)),
         dma((chunks,)),
@@ -390,8 +393,8 @@
         dma((2, chunks, slow)),
         dma((chunks,)),
         dma((chunks,)),
-        dma((half,)),
-        dma((half,)),
+        dma((half + 1,)),
+        dma((half + 1,)),
     ]
     anywhere = pl.BlockSpec(memory_space=pl.ANY)
     inside = pl.BlockSpec(memory_space=pltpu.VMEM)

time: 80.6 us -> 82.2 us (1.020)
  Pallas kernels: 77.3 us -> 78.9 us
    pallas_call x1, Pallas kernels: 77.3 us -> 78.9 us  [per_device(): pl.pallas_call(functools.partial(kernel, n, pipe, cap), out_shape=(vm((ha...]
where the time goes in v3:
time: 82.2 us; the launch traced here: 82.1 us
  Pallas kernels  78.9 us (96%)
  local copies, waits for them, and re-layouts  2.55 us (3%)
    pallas_call x1, Pallas kernels, per_device(): pl.pallas_call(functools.partial(kernel, n, pipe, cap), out_shape=(vm((ha...  78.9 us
    unnamed x2, local copies, waits for them, and re-layouts  2.55 us

profile of v3, /device:TPU:0, one launch (start us, length us, event | category | flops | bytes accessed | tf_op | source)
XLA Modules:
  0.0 82.1 jit_solution(13933939922635804604)
XLA Ops:
  0.6 78.9 %shard_map.59 = (bf16[2,768,1024]{2,1,0:T(8,128)(2,1)S(1)}, bf16[128,3072]{1,0:T(8,128)(2,1)S(1)}) custom-call(s32[2,128]{1,0:T(2,128)} %bitcast.13, bf16[128,3072]{1,0:T(8,128)(2,1)} %bitcast.11, bf16[3072,1024]{1,0:T(8,128)(2,1)} %bitcast.10, bf16[192,1024]{1,0:T(8,128)(2,1)} %bitcast.12), custom_call_target="tpu_custom_call" | custom-call | flops 3623878656 | bytes 11010048 | tf_op jit(solution)/shard_map/pallas_call | solution.py:401
  79.5 1.7 %copy.8 = bf16[1,1536,1024]{2,1,0:T(8,128)(2,1)} copy(bf16[1,1536,1024]{2,1,0:T(8,128)(2,1)S(1)} %bitcast.8) | data formatting | bytes 6291456
  81.2 0.9 %copy.9 = bf16[1,1,128,3072]{3,2,1,0:T(8,128)(2,1)} copy(bf16[1,1,128,3072]{3,2,1,0:T(8,128)(2,1)S(1)} %bitcast.9) | data formatting | bytes 1572864

commit v4 on v3

v4 whole, which is shorter than its diff:
```python
import functools

import jax
import jax.numpy as jnp
from jax import lax
from jax.experimental import pallas as pl
from jax.experimental.pallas import tpu as pltpu
from jax.sharding import PartitionSpec as P

MESH = pl.DeviceIdType.MESH
F32 = jnp.float32
BF16 = jnp.bfloat16
CHUNKS = 4


def factors(n):
    fast = 1
    while (fast * 2) ** 2 <= n:
        fast *= 2
    return n // fast, fast


def kernel(
    n, pipe, cap,
    routes_hbm, acts_hbm, weight_hbm, cot_hbm,
    w_sum, spread,
    ids, acts, weight, cot, compacted, gathered, rows, rows_out, acc, pre_grad,
    own_term, y_out, y_in, z_out, z_in, done, back,
    local_sem, ids_sem, x_send, g_recv, gs_send, gf_send, y_send, y_recv, z_send, z_recv,
    b_send, b_recv, f_send, f_recv,
):
    chunks = CHUNKS
    slow, fast = factors(n)
    p, f, r = lax.axis_index("pipe"), lax.axis_index("fsdp"), lax.axis_index("rep")
    a, b = f // fast, lax.rem(f, fast)
    nxt, prv = lax.rem(p + 1, pipe), lax.rem(p + pipe - 1, pipe)
    slots = n * cap
    dc = weight.shape[1]
    half = chunks // 2

    def peer(j):
        return a * fast + lax.rem(b + j, fast)

    def ahead(k):
        return lax.rem(a + k, slow)

    def behind(k):
        return lax.rem(a + slow - k, slow)

    def remote(src, dst, send, recv, where):
        return pltpu.make_async_remote_copy(
            src_ref=src, dst_ref=dst, send_sem=send, recv_sem=recv,
            device_id=where, device_id_type=MESH,
        )

    def greet(where):
        pl.semaphore_signal(barrier, inc=1, device_id=where, device_id_type=MESH)

    acts_load = pltpu.make_async_copy(acts_hbm, acts, local_sem.at[0])
    acts_load.start()
    barrier = pltpu.get_barrier_semaphore()
    greet({"pipe": prv})
    if pipe > 2:
        greet({"pipe": nxt})
    greet({"rep": 1 - r})
    for j in range(1, fast):
        greet({"fsdp": peer(j)})

    for k in range(1, slow):
        greet({"fsdp": ahead(k) * fast + b})

    weight_loads = []
    for c in range(chunks):
        load = pltpu.make_async_copy(
            weight_hbm.at[pl.ds(c * dc, dc)], weight.at[c], local_sem.at[2 + c]
        )
        load.start()
        weight_loads.append(load)
    cot_load = pltpu.make_async_copy(cot_hbm, cot, local_sem.at[1])
    cot_load.start()

    pl.semaphore_wait(barrier, (1 if pipe == 2 else 2) + 1 + (fast - 1) + (slow - 1))

    ids_copy = remote(routes_hbm, ids, ids_sem.at[0], ids_sem.at[1], {"pipe": prv})
    ids_copy.start()
    ids_copy.wait_recv()
    tokens = ids.shape[1]
    named = jnp.where(ids[...] == 0, 1.0, 0.0).astype(F32)
    chosen = jnp.max(named, axis=0, keepdims=True)
    row = lax.broadcasted_iota(jnp.int32, (tokens, tokens), 0)
    col = lax.broadcasted_iota(jnp.int32, (tokens, tokens), 1)
    before = jnp.where(row <= col, 1.0, 0.0).astype(BF16)
    chosen8 = jnp.broadcast_to(chosen, (16, tokens))
    ordinal = jnp.dot(chosen8.astype(BF16), before, preferred_element_type=F32)[0:1] - 1.0
    hits = jnp.where(
        (jnp.broadcast_to(ordinal, (tokens, tokens)) == row.astype(F32))
        & (jnp.broadcast_to(chosen, (tokens, tokens)) > 0.5),
        1.0, 0.0,
    ).astype(F32)
    picker = hits[0:cap].astype(BF16)
    spreader = hits.T.astype(BF16)
    acts_load.wait()

    def x_copy(c):
        return remote(
            compacted.at[c], gathered.at[c, f], x_send.at[c], g_recv.at[c, f], {"pipe": nxt}
        )

    for c in range(chunks):
        compacted[c] = jnp.dot(
            picker, acts[:, c * dc:(c + 1) * dc], preferred_element_type=F32
        ).astype(BF16)
        x_copy(c).start()

    def g_wait(c, block):
        remote(
            gathered.at[c, block], gathered.at[c, block],
            gs_send.at[c, 0], g_recv.at[c, block], {"pipe": nxt},
        ).wait_recv()

    def slow_copy(c, k):
        return remote(
            gathered.at[c, f], gathered.at[c, f], gs_send.at[c, k - 1], g_recv.at[c, f],
            {"fsdp": behind(k) * fast + b},
        )

    def fast_copy(c, k, j):
        block = ahead(k) * fast + b
        return remote(
            gathered.at[c, block], gathered.at[c, block], gf_send.at[c, k, j - 1],
            g_recv.at[c, block], {"fsdp": peer(j)},
        )

    def send_own(c):
        g_wait(c, f)
        for j in range(1, fast):
            fast_copy(c, 0, j).start()
        for k in range(1, slow):
            slow_copy(c, k).start()

    def pass_on(c):
        for k in range(1, slow):
            g_wait(c, ahead(k) * fast + b)
            for j in range(1, fast):
                fast_copy(c, k, j).start()

    def rows_copy(i):
        return remote(rows_out.at[i], rows.at[i, 1], f_send.at[i], f_recv.at[i], {"rep": 1 - r})

    grad_copy = remote(
        pre_grad.at[0], pre_grad.at[1], f_send.at[half], f_recv.at[half], {"rep": 1 - r}
    )

    def first_matmul(c):
        for k in range(slow):
            for j in range(1, fast):
                g_wait(c, ahead(k) * fast + lax.rem(b + j, fast))
        block = gathered[c].astype(F32).reshape(slots, dc).astype(BF16)
        i, mine = c % half, r == c // half

        @pl.when(mine)
        def _():
            rows[i, 0] = block

        @pl.when(jnp.logical_not(mine))
        def _():
            rows_out[i] = block
            rows_copy(i).start()

        weight_loads[c].wait()
        part = jnp.dot(block, weight[c], preferred_element_type=F32)
        if c == 0:
            acc[...] = part
        else:
            acc[...] += part

    for c in range(chunks):
        send_own(c)
    pass_on(0)
    for c in range(chunks):
        if c + 1 < chunks:
            pass_on(c + 1)
        first_matmul(c)

    cot_load.wait()
    piece = 48
    for i in range(slots // piece):
        span = pl.ds(i * piece, piece)
        pre = acc[span]
        s = jax.nn.sigmoid(pre)
        pre_grad[0, span] = (cot[span].astype(F32) * s * (1.0 + pre * (1.0 - s))).astype(BF16)
    grad_copy.start()

    def y_copy(c, j, k):
        to, dest = lax.rem(b + j, fast), behind(k)
        return remote(
            y_out.at[c, to, dest], y_in.at[c, j - 1, dest], y_send.at[c, j - 1, k],
            y_recv.at[c, j - 1, k], {"fsdp": peer(j)},
        )

    def slot_matmul(c):
        term = lax.dot_general(
            pre_grad[0], weight[c], (((1,), (1,)), ((), ())), preferred_element_type=F32
        ).reshape(n, cap, dc)
        own_term[c] = term
        for aa in range(slow):
            for bb in range(fast):
                y_out[c, bb, aa] = term[aa * fast + bb].astype(BF16)
        for k in [*range(1, slow), 0]:
            for j in range(1, fast):
                y_copy(c, j, k).start()

    def partial(c, k):
        dest = behind(k)
        value = own_term[c, dest * fast + b]
        for j in range(1, fast):
            y_copy(c, j, k).wait_recv()
            value = value + y_in[c, j - 1, dest].astype(F32)
        return value

    def z_copy(c, k):
        return remote(
            z_out.at[c, k - 1], z_in.at[c, k - 1], z_send.at[c, k - 1], z_recv.at[c, k - 1],
            {"fsdp": behind(k) * fast + b},
        )

    def send_partials(c):
        for k in range(1, slow):
            z_out[c, k - 1] = partial(c, k).astype(BF16)
            z_copy(c, k).start()

    def back_copy(c):
        return remote(done.at[c], back.at[c], b_send.at[c], b_recv.at[c], {"pipe": prv})

    def finish(c):
        total = partial(c, 0)
        for k in range(1, slow):
            z_copy(c, k).wait_recv()
            total = total + z_in[c, k - 1].astype(F32)
        done[c] = total.astype(BF16)
        back_copy(c).start()

    parts = 3
    depth = dc // parts

    def weight_tile(i, part):
        if part == 0:
            rows_copy(i).wait_recv()
            if i == 0:
                grad_copy.wait_recv()
        span = slice(part * depth, (part + 1) * depth)
        w_sum[i, span] = lax.dot_general(
            rows[i, :, :, span].reshape(2 * slots, depth), pre_grad[...].reshape(2 * slots, -1),
            (((0,), (0,)), ((), ())), preferred_element_type=F32,
        ).astype(BF16)

    def put_back(c):
        back_copy(c).wait_recv()
        grads = back[c].astype(F32)
        padded = jnp.concatenate(
            [grads, jnp.zeros((tokens - cap, dc), F32)], axis=0
        ).astype(BF16)
        spread[:, c * dc:(c + 1) * dc] = jnp.dot(
            spreader, padded, preferred_element_type=F32
        ).astype(BF16)

    beside = [functools.partial(weight_tile, i, j) for i in range(half) for j in range(parts)]
    beside.reverse()
    for c in range(chunks):
        slot_matmul(c)
        if c:
            send_partials(c - 1)
    beside.pop()()
    finish(0)
    send_partials(chunks - 1)
    for c in range(1, chunks):
        if beside:
            beside.pop()()
        finish(c)
    for c in range(chunks - 1):
        if beside:
            beside.pop()()
        put_back(c)
    while beside:
        beside.pop()()
    put_back(chunks - 1)

    ids_copy.wait_send()
    for c in range(chunks):
        x_copy(c).wait_send()
        for k in range(slow):
            for j in range(1, fast):
                fast_copy(c, k, j).wait_send()
                y_copy(c, j, k).wait_send()
            if k:
                slow_copy(c, k).wait_send()
                z_copy(c, k).wait_send()
        back_copy(c).wait_send()
    for i in range(half):
        rows_copy(i).wait_send()
    grad_copy.wait_send()


def per_device(section_acts, route_ids, gate_weight, hidden_cot):
    n, pipe = lax.axis_size("fsdp"), lax.axis_size("pipe")
    acts, weight, cot = section_acts[0, 0], gate_weight[0], hidden_cot[0, 0]
    routes = route_ids[0, 0].T
    tokens, width = acts.shape
    slots, hidden = cot.shape
    cap = slots // n
    slow, fast = factors(n)
    chunks, half = CHUNKS, CHUNKS // 2
    dc = width // chunks
    peers, hops = max(fast - 1, 1), max(slow - 1, 1)
    dma = pltpu.SemaphoreType.DMA
    vm = pltpu.VMEM
    scratch = [
        vm(routes.shape, jnp.int32),
        vm((tokens, width), BF16),
        vm((chunks, dc, hidden), BF16),
        vm((slots, hidden), BF16),
        vm((chunks, cap, dc), BF16),
        vm((chunks, n, cap, dc), BF16),
        vm((half, 2, slots, dc), BF16),
        vm((half, slots, dc), BF16),
        vm((slots, hidden), F32),
        vm((2, slots, hidden), BF16),
        vm((chunks, n, cap, dc), F32),
        vm((chunks, fast, slow, cap, dc), BF16),
        vm((chunks, peers, slow, cap, dc), BF16),
        vm((chunks, hops, cap, dc), BF16),
        vm((chunks, hops, cap, dc), BF16),
        vm((chunks, cap, dc), BF16),
        vm((chunks, cap, dc), BF16),
        dma((2 + chunks,)),
        dma((2,)),
        dma((chunks,)),
        dma((chunks, n)),
        dma((chunks, hops)),
        dma((chunks, slow, peers)),
        dma((chunks, peers, slow)),
        dma((chunks, peers, slow)),
        dma((chunks, hops)),
        dma((chunks, hops)),
        dma((chunks,)),
        dma((chunks,)),
        dma((half + 1,)),
        dma((half + 1,)),
    ]
    anywhere = pl.BlockSpec(memory_space=pl.ANY)
    inside = pl.BlockSpec(memory_space=pltpu.VMEM)
    weight_grad, acts_grad = pl.pallas_call(
        functools.partial(kernel, n, pipe, cap),
        out_shape=(
            vm((half, dc, hidden), BF16),
            vm((tokens, width), BF16),
        ),
        in_specs=[anywhere] * 4,
        out_specs=(inside, inside),
        scratch_shapes=scratch,
        compiler_params=pltpu.CompilerParams(
            collective_id=0, has_side_effects=True, vmem_limit_bytes=56 * 1024 * 1024
        ),
        cost_estimate=pl.CostEstimate(
            flops=6 * slots * width * hidden,
            bytes_accessed=3 * width * hidden + 4 * tokens * width,
            transcendentals=slots * hidden,
        ),
    )(routes, acts, weight, cot)
    return (weight_grad.reshape(1, width // 2, hidden), acts_grad[None, None])


def solution(mesh):
    return jax.shard_map(
        per_device,
        mesh=mesh,
        in_specs=(
            P("pipe", "rep", "fsdp", None),
            P("pipe", "rep", "fsdp", None),
            P("pipe", None, "fsdp"),
            P("pipe", "rep", None, "fsdp"),
        ),
        out_specs=(P("pipe", "rep", "fsdp"), P("pipe", "rep", "fsdp", None)),
        check_vma=False,
    )
```

time: 82.2 us -> 55.2 us (0.67)
  Pallas kernels: 78.9 us -> 51.9 us
    pallas_call x1, Pallas kernels: 78.9 us -> 51.9 us  [per_device(): pl.pallas_call(functools.partial(kernel, n, pipe, cap), out_shape=(vm((ha...]
where the time goes in v4:
time: 55.2 us; the launch traced here: 55.1 us
  Pallas kernels  51.9 us (94%)
  local copies, waits for them, and re-layouts  2.55 us (5%)
  between operations  0.64 us (1%)
    pallas_call x1, Pallas kernels, per_device(): pl.pallas_call(functools.partial(kernel, n, pipe, cap), out_shape=(vm((ha...  51.9 us
    unnamed x2, local copies, waits for them, and re-layouts  2.55 us

profile of v4, /device:TPU:0, one launch (start us, length us, event | category | flops | bytes accessed | tf_op | source)
XLA Modules:
  0.0 55.1 jit_solution(8800615678902570344)
XLA Ops:
  0.6 51.9 %shard_map.59 = (bf16[2,768,1024]{2,1,0:T(8,128)(2,1)S(1)}, bf16[128,3072]{1,0:T(8,128)(2,1)S(1)}) custom-call(s32[2,128]{1,0:T(2,128)} %bitcast.13, bf16[128,3072]{1,0:T(8,128)(2,1)} %bitcast.11, bf16[3072,1024]{1,0:T(8,128)(2,1)} %bitcast.10, bf16[192,1024]{1,0:T(8,128)(2,1)} %bitcast.12), custom_call_target="tpu_custom_call" | custom-call | flops 3623878656 | bytes 11010048 | tf_op jit(solution)/shard_map/pallas_call | solution.py:352
  52.5 1.7 %copy.8 = bf16[1,1536,1024]{2,1,0:T(8,128)(2,1)} copy(bf16[1,1536,1024]{2,1,0:T(8,128)(2,1)S(1)} %bitcast.8) | data formatting | bytes 6291456
  54.2 0.9 %copy.9 = bf16[1,1,128,3072]{3,2,1,0:T(8,128)(2,1)} copy(bf16[1,1,128,3072]{3,2,1,0:T(8,128)(2,1)S(1)} %bitcast.9) | data formatting | bytes 1572864

commit v5 on v4

--- a/solution.py
+++ b/solution.py
@@ -25,9 +25,9 @@
     routes_hbm, acts_hbm, weight_hbm, cot_hbm,
     w_sum, spread,
     ids, acts, weight, cot, compacted, gathered, rows, rows_out, acc, pre_grad,
-    own_term, y_out, y_in, z_out, z_in, done, back,
-    local_sem, ids_sem, x_send, g_recv, gs_send, gf_send, y_send, y_recv, z_send, z_recv,
-    b_send, b_recv, f_send, f_recv,
+    own_term, y_out, y_in, z_out, z_in,
+    local_sem, ids_sem, x_send, g_recv, gf_send, y_send, y_recv, z_send, z_recv,
+    f_send, f_recv,
 ):
     chunks = CHUNKS
     slow, fast = factors(n)
@@ -59,15 +59,13 @@
     acts_load = pltpu.make_async_copy(acts_hbm, acts, local_sem.at[0])
     acts_load.start()
     barrier = pltpu.get_barrier_semaphore()
-    greet({"pipe": prv})
-    if pipe > 2:
-        greet({"pipe": nxt})
+    for k in range(slow):
+        greet({"pipe": prv, "fsdp": ahead(k) * fast + b})
+        if pipe > 2:
+            greet({"pipe": nxt, "fsdp": ahead(k) * fast + b})
     greet({"rep": 1 - r})
     for j in range(1, fast):
         greet({"fsdp": peer(j)})
-
-    for k in range(1, slow):
-        greet({"fsdp": ahead(k) * fast + b})
 
     weight_loads = []
     for c in range(chunks):
@@ -79,7 +77,7 @@
     cot_load = pltpu.make_async_copy(cot_hbm, cot, local_sem.at[1])
     cot_load.start()
 
-    pl.semaphore_wait(barrier, (1 if pipe == 2 else 2) + 1 + (fast - 1) + (slow - 1))
+    pl.semaphore_wait(barrier, (1 if pipe == 2 else 2) * slow + fast)
 
     ids_copy = remote(routes_hbm, ids, ids_sem.at[0], ids_sem.at[1], {"pipe": prv})
     ids_copy.start()
@@ -101,28 +99,24 @@
     spreader = hits.T.astype(BF16)
     acts_load.wait()
 
-    def x_copy(c):
+    def x_copy(c, k):
         return remote(
-            compacted.at[c], gathered.at[c, f], x_send.at[c], g_recv.at[c, f], {"pipe": nxt}
+            compacted.at[c], gathered.at[c, f], x_send.at[c, k], g_recv.at[c, f],
+            {"pipe": nxt, "fsdp": behind(k) * fast + b},
         )
 
     for c in range(chunks):
         compacted[c] = jnp.dot(
             picker, acts[:, c * dc:(c + 1) * dc], preferred_element_type=F32
         ).astype(BF16)
-        x_copy(c).start()
+        for k in range(slow):
+            x_copy(c, k).start()
 
     def g_wait(c, block):
         remote(
             gathered.at[c, block], gathered.at[c, block],
-            gs_send.at[c, 0], g_recv.at[c, block], {"pipe": nxt},
+            x_send.at[c, 0], g_recv.at[c, block], {"pipe": nxt},
         ).wait_recv()
-
-    def slow_copy(c, k):
-        return remote(
-            gathered.at[c, f], gathered.at[c, f], gs_send.at[c, k - 1], g_recv.at[c, f],
-            {"fsdp": behind(k) * fast + b},
-        )
 
     def fast_copy(c, k, j):
         block = ahead(k) * fast + b
@@ -131,15 +125,8 @@
             g_recv.at[c, block], {"fsdp": peer(j)},
         )
 
-    def send_own(c):
-        g_wait(c, f)
-        for j in range(1, fast):
-            fast_copy(c, 0, j).start()
-        for k in range(1, slow):
-            slow_copy(c, k).start()
-
     def pass_on(c):
-        for k in range(1, slow):
+        for k in range(slow):
             g_wait(c, ahead(k) * fast + b)
             for j in range(1, fast):
                 fast_copy(c, k, j).start()
@@ -174,8 +161,6 @@
         else:
             acc[...] += part
 
-    for c in range(chunks):
-        send_own(c)
     pass_on(0)
     for c in range(chunks):
         if c + 1 < chunks:
@@ -220,25 +205,14 @@
 
     def z_copy(c, k):
         return remote(
-            z_out.at[c, k - 1], z_in.at[c, k - 1], z_send.at[c, k - 1], z_recv.at[c, k - 1],
-            {"fsdp": behind(k) * fast + b},
+            z_out.at[c, k], z_in.at[c, k], z_send.at[c, k], z_recv.at[c, k],
+            {"pipe": prv, "fsdp": behind(k) * fast + b},
         )
 
     def send_partials(c):
-        for k in range(1, slow):
-            z_out[c, k - 1] = partial(c, k).astype(BF16)
+        for k in [*range(1, slow), 0]:
+            z_out[c, k] = partial(c, k).astype(BF16)
             z_copy(c, k).start()
-
-    def back_copy(c):
-        return remote(done.at[c], back.at[c], b_send.at[c], b_recv.at[c], {"pipe": prv})
-
-    def finish(c):
-        total = partial(c, 0)
-        for k in range(1, slow):
-            z_copy(c, k).wait_recv()
-            total = total + z_in[c, k - 1].astype(F32)
-        done[c] = total.astype(BF16)
-        back_copy(c).start()
 
     parts = 3
     depth = dc // parts
@@ -255,8 +229,11 @@
         ).astype(BF16)
 
     def put_back(c):
-        back_copy(c).wait_recv()
-        grads = back[c].astype(F32)
+        grads = jnp.zeros((cap, dc), F32)
+        for k in range(slow):
+            z_copy(c, k).wait_recv()
+            grads = grads + z_in[c, k].astype(F32)
+        grads = grads.astype(BF16).astype(F32)
         padded = jnp.concatenate(
             [grads, jnp.zeros((tokens - cap, dc), F32)], axis=0
         ).astype(BF16)
@@ -268,34 +245,31 @@
     beside.reverse()
     for c in range(chunks):
         slot_matmul(c)
+        if c == chunks - 1:
+            beside.pop()()
         if c:
             send_partials(c - 1)
     beside.pop()()
-    finish(0)
+    put_back(0)
+    if beside:
+        beside.pop()()
     send_partials(chunks - 1)
     for c in range(1, chunks):
         if beside:
             beside.pop()()
-        finish(c)
-    for c in range(chunks - 1):
-        if beside:
-            beside.pop()()
+        if c == chunks - 1:
+            while beside:
+                beside.pop()()
         put_back(c)
-    while beside:
-        beside.pop()()
-    put_back(chunks - 1)
 
     ids_copy.wait_send()
     for c in range(chunks):
-        x_copy(c).wait_send()
         for k in range(slow):
             for j in range(1, fast):
                 fast_copy(c, k, j).wait_send()
                 y_copy(c, j, k).wait_send()
-            if k:
-                slow_copy(c, k).wait_send()
-                z_copy(c, k).wait_send()
-        back_copy(c).wait_send()
+            x_copy(c, k).wait_send()
+            z_copy(c, k).wait_send()
     for i in range(half):
         rows_copy(i).wait_send()
     grad_copy.wait_send()
@@ -311,7 +285,7 @@
     slow, fast = factors(n)
     chunks, half = CHUNKS, CHUNKS // 2
     dc = width // chunks
-    peers, hops = max(fast - 1, 1), max(slow - 1, 1)
+    peers = max(fast - 1, 1)
     dma = pltpu.SemaphoreType.DMA
     vm = pltpu.VMEM
     scratch = [
@@ -328,22 +302,17 @@
         vm((chunks, n, cap, dc), F32),
         vm((chunks, fast, slow, cap, dc), BF16),
         vm((chunks, peers, slow, cap, dc), BF16),
-        vm((chunks, hops, cap, dc), BF16),
-        vm((chunks, hops, cap, dc), BF16),
-        vm((chunks, cap, dc), BF16),
-        vm((chunks, cap, dc), BF16),
+        vm((chunks, slow, cap, dc), BF16),
+        vm((chunks, slow, cap, dc), BF16),
         dma((2 + chunks,)),
         dma((2,)),
-        dma((chunks,)),
+        dma((chunks, slow)),
         dma((chunks, n)),
-        dma((chunks, hops)),
         dma((chunks, slow, peers)),
         dma((chunks, peers, slow)),
         dma((chunks, peers, slow)),
-        dma((chunks, hops)),
-        dma((chunks, hops)),
-        dma((chunks,)),
-        dma((chunks,)),
+        dma((chunks, slow)),
+        dma((chunks, slow)),
         dma((half + 1,)),
         dma((half + 1,)),
     ]

time: 55.2 us -> 55.8 us (1.011)
  Pallas kernels: 51.9 us -> 52.5 us
    pallas_call x1, Pallas kernels: 51.9 us -> 52.5 us  [per_device(): pl.pallas_call(functools.partial(kernel, n, pipe, cap), out_shape=(vm((ha...]
where the time goes in v5:
time: 55.8 us; the launch traced here: 55.6 us
  Pallas kernels  52.5 us (94%)
  local copies, waits for them, and re-layouts  2.55 us (5%)
  between operations  0.64 us (1%)
    pallas_call x1, Pallas kernels, per_device(): pl.pallas_call(functools.partial(kernel, n, pipe, cap), out_shape=(vm((ha...  52.5 us
    unnamed x2, local copies, waits for them, and re-layouts  2.55 us

profile of v5, /device:TPU:0, one launch (start us, length us, event | category | flops | bytes accessed | tf_op | source)
XLA Modules:
  0.0 55.6 jit_solution(2338157233803959994)
XLA Ops:
  0.6 52.5 %shard_map.59 = (bf16[2,768,1024]{2,1,0:T(8,128)(2,1)S(1)}, bf16[128,3072]{1,0:T(8,128)(2,1)S(1)}) custom-call(s32[2,128]{1,0:T(2,128)} %bitcast.13, bf16[128,3072]{1,0:T(8,128)(2,1)} %bitcast.11, bf16[3072,1024]{1,0:T(8,128)(2,1)} %bitcast.10, bf16[192,1024]{1,0:T(8,128)(2,1)} %bitcast.12), custom_call_target="tpu_custom_call" | custom-call | flops 3623878656 | bytes 11010048 | tf_op jit(solution)/shard_map/pallas_call | solution.py:321
  53.1 1.7 %copy.8 = bf16[1,1536,1024]{2,1,0:T(8,128)(2,1)} copy(bf16[1,1536,1024]{2,1,0:T(8,128)(2,1)S(1)} %bitcast.8) | data formatting | bytes 6291456
  54.8 0.9 %copy.9 = bf16[1,1,128,3072]{3,2,1,0:T(8,128)(2,1)} copy(bf16[1,1,128,3072]{3,2,1,0:T(8,128)(2,1)S(1)} %bitcast.9) | data formatting | bytes 1572864

commit v6 on v5

--- a/solution.py
+++ b/solution.py
@@ -25,7 +25,7 @@
     routes_hbm, acts_hbm, weight_hbm, cot_hbm,
     w_sum, spread,
     ids, acts, weight, cot, compacted, gathered, rows, rows_out, acc, pre_grad,
-    own_term, y_out, y_in, z_out, z_in,
+    own_term, w_acc, y_out, y_in, z_out, z_in,
     local_sem, ids_sem, x_send, g_recv, gf_send, y_send, y_recv, z_send, z_recv,
     f_send, f_recv,
 ):
@@ -214,19 +214,26 @@
             z_out[c, k] = partial(c, k).astype(BF16)
             z_copy(c, k).start()
 
-    parts = 3
+    parts = 3 if dc % 3 == 0 else 1
     depth = dc // parts
 
-    def weight_tile(i, part):
+    def product(i, which, span):
+        return lax.dot_general(
+            rows[i, which, :, span], pre_grad[which], (((0,), (0,)), ((), ())),
+            preferred_element_type=F32,
+        )
+
+    def own_tile(i, part):
+        span = slice(part * depth, (part + 1) * depth)
+        w_acc[i, span] = product(i, 0, span)
+
+    def other_tile(i, part):
         if part == 0:
             rows_copy(i).wait_recv()
             if i == 0:
                 grad_copy.wait_recv()
         span = slice(part * depth, (part + 1) * depth)
-        w_sum[i, span] = lax.dot_general(
-            rows[i, :, :, span].reshape(2 * slots, depth), pre_grad[...].reshape(2 * slots, -1),
-            (((0,), (0,)), ((), ())), preferred_element_type=F32,
-        ).astype(BF16)
+        w_sum[i, span] = (w_acc[i, span] + product(i, 1, span)).astype(BF16)
 
     def put_back(c):
         grads = jnp.zeros((cap, dc), F32)
@@ -241,25 +248,22 @@
             spreader, padded, preferred_element_type=F32
         ).astype(BF16)
 
-    beside = [functools.partial(weight_tile, i, j) for i in range(half) for j in range(parts)]
-    beside.reverse()
+    tiles = [(i, j) for i in range(half) for j in range(parts)]
+    own = [functools.partial(own_tile, *tile) for tile in reversed(tiles)]
+    others = [functools.partial(other_tile, *tile) for tile in reversed(tiles)]
     for c in range(chunks):
         slot_matmul(c)
-        if c == chunks - 1:
-            beside.pop()()
         if c:
+            own.pop()()
             send_partials(c - 1)
-    beside.pop()()
-    put_back(0)
-    if beside:
-        beside.pop()()
+    own.pop()()
     send_partials(chunks - 1)
-    for c in range(1, chunks):
-        if beside:
-            beside.pop()()
-        if c == chunks - 1:
-            while beside:
-                beside.pop()()
+    while own:
+        own.pop()()
+    for c in range(chunks):
+        share = 1 if c == 0 else 2
+        for _ in range(len(others) if c == chunks - 1 else min(share, len(others))):
+            others.pop()()
         put_back(c)
 
     ids_copy.wait_send()
@@ -300,6 +304,7 @@
         vm((slots, hidden), F32),
         vm((2, slots, hidden), BF16),
         vm((chunks, n, cap, dc), F32),
+        vm((half, dc, hidden), F32),
         vm((chunks, fast, slow, cap, dc), BF16),
         vm((chunks, peers, slow, cap, dc), BF16),
         vm((chunks, slow, cap, dc), BF16),

time: 55.8 us -> 55.4 us (level)
  no operation moved by 1% of the time
where the time goes in v6:
time: 55.4 us; the launch traced here: 55.2 us
  Pallas kernels  52.1 us (94%)
  local copies, waits for them, and re-layouts  2.55 us (5%)
  between operations  0.64 us (1%)
    pallas_call x1, Pallas kernels, per_device(): pl.pallas_call(functools.partial(kernel, n, pipe, cap), out_shape=(vm((ha...  52.1 us
    unnamed x2, local copies, waits for them, and re-layouts  2.55 us

profile of v6, /device:TPU:0, one launch (start us, length us, event | category | flops | bytes accessed | tf_op | source)
XLA Modules:
  0.0 55.2 jit_solution(8982385334504234113)
XLA Ops:
  0.6 52.1 %shard_map.59 = (bf16[2,768,1024]{2,1,0:T(8,128)(2,1)S(1)}, bf16[128,3072]{1,0:T(8,128)(2,1)S(1)}) custom-call(s32[2,128]{1,0:T(2,128)} %bitcast.13, bf16[128,3072]{1,0:T(8,128)(2,1)} %bitcast.11, bf16[3072,1024]{1,0:T(8,128)(2,1)} %bitcast.10, bf16[192,1024]{1,0:T(8,128)(2,1)} %bitcast.12), custom_call_target="tpu_custom_call" | custom-call | flops 3623878656 | bytes 11010048 | tf_op jit(solution)/shard_map/pallas_call | solution.py:326
  52.7 1.7 %copy.8 = bf16[1,1536,1024]{2,1,0:T(8,128)(2,1)} copy(bf16[1,1536,1024]{2,1,0:T(8,128)(2,1)S(1)} %bitcast.8) | data formatting | bytes 6291456
  54.4 0.9 %copy.9 = bf16[1,1,128,3072]{3,2,1,0:T(8,128)(2,1)} copy(bf16[1,1,128,3072]{3,2,1,0:T(8,128)(2,1)S(1)} %bitcast.9) | data formatting | bytes 1572864
